TPU v7x, 256 devices: a whole 4x4x8 slice. The times are simulated.
256 devices in a mesh: hist: 32 (over z, y), orow: 2 (over x_lo), ocol: 4 (over x_hi, core).
Axes of the slice: x: 4 (x_hi: 2, x_lo: 2; x = x_hi * 2 + x_lo), y: 4, z: 8, core: 2. Of those that a mesh axis runs over, the one named last changes fastest.
Arguments:
- lesser_hist: float32 [2, 128, 256, 256], P(None, 'hist', 'ocol', 'orow'), may hold values from -6 to 6
- greater_hist: float32 [2, 128, 256, 256], P(None, 'hist', 'orow', 'ocol'), may hold values from -6 to 6
- advanced_hist: float32 [2, 128, 32, 256, 256], P(None, 'hist', 'ocol', None, 'orow'), may hold values from -6 to 6
- current_row: float32 [2, 32, 256, 256], P(None, 'ocol', 'hist', 'orow'), may hold values from -6 to 6
- adjacency: int32 [256, 256], P('hist'), may hold values from 0 to 1, as said below
- weight_table: int32 [128], P('hist'), may hold values from 1 to 48
- step_index: int32 [1], replicated, may hold values from 32 to 127
Outputs:
- new_row: float32 [2, 32, 256, 256], P(None, 'ocol', 'hist', 'orow')
Inputs may be any that keep to these rules, and one draw needn't show every extreme that they name: `adjacency`: symmetric, zero on the diagonal.
All inputs are finite; a program needn't handle non-finite values.
Results may differ from a plain program's by a relative error of at most 0.0001.
Values sent between devices are 32-bit elements; how exact they have to be, the bound alone decides.
A program may use at most 64 MiB of HBM per device.

v0:
```python
import jax
import jax.numpy as jnp
from jax import lax
from jax.sharding import PartitionSpec as P

coupling_square = 0.25
hopping = 4.0
time_step = 0.01


def self_energy(lesser, greater_t):
    lesser_re, lesser_im = (lesser[0], lesser[1])
    greater_re, greater_im = (greater_t[0], greater_t[1])
    square_re = lesser_re * lesser_re - lesser_im * lesser_im
    square_im = 2.0 * lesser_re * lesser_im
    sigma_re = coupling_square * (square_re * greater_re - square_im * greater_im)
    sigma_im = coupling_square * (square_re * greater_im + square_im * greater_re)
    return jnp.stack([sigma_re, sigma_im])


def on_device(
    lesser_hist, greater_hist, advanced_hist, current_row, adjacency, weight_table, step_index
):
    slices_here = lesser_hist.shape[1]
    slot_ids = lax.axis_index("hist") * slices_here + lax.iota(jnp.int32, slices_here)
    weights = jnp.where(
        slot_ids <= step_index[0], weight_table.astype(jnp.float32) / 24.0, jnp.float32(0.0)
    )
    lesser_full, greater_full = (
        lax.all_gather(lesser_hist, "ocol", axis=2, tiled=True),
        lax.all_gather(greater_hist, "ocol", axis=3, tiled=True),
    )
    lesser_full, greater_full = (
        lax.all_gather(lesser_full, "orow", axis=3, tiled=True),
        lax.all_gather(greater_full, "orow", axis=2, tiled=True),
    )
    sigma = self_energy(lesser_full, jnp.swapaxes(greater_full, 2, 3))
    sigma_w = sigma * weights[None, :, None, None]
    combos = jnp.einsum(
        "csik,dstkj->cdtij",
        sigma_w,
        advanced_hist,
        precision=lax.Precision.HIGHEST,
        preferred_element_type=jnp.float32,
    )
    collision = jnp.stack([combos[0, 0] - combos[1, 1], combos[0, 1] + combos[1, 0]])
    hop_local = -hopping * adjacency.astype(jnp.float32)
    summed = lax.psum_scatter(collision, "hist", scatter_dimension=2, tiled=True)
    row_full = lax.all_gather(current_row, "hist", axis=2, tiled=True)
    summed = summed + jnp.einsum(
        "ik,ctkj->ctij",
        hop_local,
        row_full,
        precision=lax.Precision.HIGHEST,
        preferred_element_type=jnp.float32,
    )
    return jnp.stack(
        [current_row[0] + time_step * summed[1], current_row[1] - time_step * summed[0]]
    )


def solution(mesh):
    in_specs = (
        P(None, "hist", "ocol", "orow"),
        P(None, "hist", "orow", "ocol"),
        P(None, "hist", "ocol", None, "orow"),
        P(None, "ocol", "hist", "orow"),
        P("hist", None),
        P("hist"),
        P(),
    )
    out_specs = P(None, "ocol", "hist", "orow")
    return jax.shard_map(
        on_device, mesh=mesh, in_specs=in_specs, out_specs=out_specs, check_vma=False
    )
```

profile of v0, /device:TPU:32, one launch (start us, length us, event | category | flops | bytes accessed | tf_op | source)
XLA Modules:
  0.0 446.7 jit_solution(13432852120616821446)
XLA Ops:
  6.5 0.0 copy-start.2
  6.5 0.0 all-gather.6.cloned.1.call-start
  6.5 0.7 all-gather.6.cloned.1.call-update
  7.3 0.0 all-gather.10.cloned.1.call-start
  7.3 0.7 all-gather.10.cloned.1.call-update
  8.0 0.0 all-gather.8.cloned.1.call-start
  8.1 27.1 %all-gather.6.cloned.1.call-done = f32[2,4,256,128]{3,2,1,0:T(8,128)} async-done(((f32[2,4,64,128]{3,2,1,0:T(8,128)}), f32[2,4,256,128]{3,2,1,0:T(8,128)}) %all-gather.6.cloned.1.call-update) | async-done | bytes 1048592 | tf_op jit(solution)/shard_map/all_gather | solution.py:30
  35.1 0.0 all-gather.8.cloned.1.call-update
  35.1 0.0 all-gather.12.cloned.1.call-start
  35.2 24.6 %all-gather.10.cloned.1.call-done = f32[2,4,128,256]{2,3,1,0:T(8,128)} async-done(((f32[2,4,128,64]{2,3,1,0:T(8,128)}), f32[2,4,128,256]{2,3,1,0:T(8,128)}) %all-gather.10.cloned.1.call-update) | async-done | bytes 1048592 | tf_op jit(solution)/shard_map/all_gather | solution.py:31
  59.8 0.0 all-gather.12.cloned.1.call-update
  59.8 0.0 all-gather.14.cloned.1.call-start
  59.8 0.5 all-gather.14.cloned.1.call-update
  60.4 0.0 reduce-scatter.2.cloned.1.call-start
  61.1 0.0 copy-done.2
  61.1 38.1 %all-gather.8.cloned.1.call-done = f32[2,4,256,256]{3,2,1,0:T(8,128)} async-done(((f32[2,4,256,128]{3,2,1,0:T(8,128)}), f32[2,4,256,256]{3,2,1,0:T(8,128)}) %all-gather.8.cloned.1.call-update) | async-done | bytes 2097168 | tf_op jit(solution)/shard_map/all_gather | solution.py:34
  99.2 40.8 %all-gather.12.cloned.1.call-done = f32[2,4,256,256]{2,3,1,0:T(8,128)} async-done(((f32[2,4,128,256]{2,3,1,0:T(8,128)}), f32[2,4,256,256]{2,3,1,0:T(8,128)}) %all-gather.12.cloned.1.call-update) | async-done | bytes 2097168 | tf_op jit(solution)/shard_map/all_gather | solution.py:35
  140.0 2.6 subtract_multiply_fusion
  142.7 16.0 %fusion.3 = f32[2,2,8,256,128]{4,3,2,1,0:T(8,128)S(1)} fusion(f32[2,4,8,256,128]{4,3,2,1,0:T(8,128)} %param.9, f32[1,4,256,256]{3,2,1,0:T(8,128)S(1)} %get-tuple-element.8, f32[1,4,256,256]{3,2,1,0:T(8,128)S(1)} %get-tuple-element.7, f32[4]{0:T(128)S(1)} %compare_select_fusion), kind=kOutput, calls=%fused_computation.3 | convolution fusion | flops 12885950464 | bytes 14680080 | tf_op jit(solution)/shard_map/csik,dstkj->cdtij/dot_general | solution.py:39
  158.7 0.2 fusion.12
  158.9 1.4 pad_maximum_fusion
  160.3 0.0 copy-start.1
  160.3 0.0 copy-start
  160.3 0.0 reduce-scatter.2.cloned.1.call-update
  160.4 57.7 %all-gather.14.cloned.1.call-done = f32[2,8,256,128]{3,2,1,0:T(8,128)} async-done(((f32[2,8,8,128]{3,2,1,0:T(8,128)}), f32[2,8,256,128]{3,2,1,0:T(8,128)}) %all-gather.14.cloned.1.call-update) | async-done | bytes 2097168 | tf_op jit(solution)/shard_map/all_gather | solution.py:49
  218.1 218.5 %reduce-scatter.2.cloned.1.call-done = f32[2,8,8,128]{3,2,1,0:T(8,128)} async-done(((f32[2,8,256,128]{3,2,1,0:T(8,128)}), f32[2,8,8,128]{3,2,1,0:T(8,128)}) %reduce-scatter.2.cloned.1.call-update) | async-done | bytes 65552 | tf_op jit(solution)/shard_map/reduce_scatter | solution.py:48
  436.5 0.0 copy-done.1
  436.6 2.7 fusion.10
  439.2 0.0 copy-done
  439.3 0.6 pad_maximum_fusion.1
  (2 shorter events, 0.0 us)
Async XLA Ops:
  6.5 54.5 %copy-start.2 = (s32[4]{0:T(128)S(1)}, s32[4]{0:T(128)}, u32[]{:S(2)}) copy-start(s32[4]{0:T(128)} %param.12) | copy-start | bytes 52
  6.5 28.6 %all-gather.6.cloned.1.call-start = ((), (), s32[]{:S(2)}) async-start(), calls=%async_computation.1 | async-start | bytes 1310720 | tf_op jit(solution)/shard_map/all_gather | solution.py:30
  7.3 52.5 %all-gather.10.cloned.1.call-start = ((), (), s32[]{:S(2)}) async-start(), calls=%async_computation.3 | async-start | bytes 1310720 | tf_op jit(solution)/shard_map/all_gather | solution.py:31
  8.0 91.2 %all-gather.8.cloned.1.call-start = ((), (), s32[]{:S(2)}) async-start(), calls=%async_computation.2 | async-start | bytes 3145728 | tf_op jit(solution)/shard_map/all_gather | solution.py:34
  35.1 104.9 %all-gather.12.cloned.1.call-start = ((), (), s32[]{:S(2)}) async-start(), calls=%async_computation.4 | async-start | bytes 3145728 | tf_op jit(solution)/shard_map/all_gather | solution.py:35
  59.8 158.3 %all-gather.14.cloned.1.call-start = ((), (), s32[]{:S(2)}) async-start(), calls=%async_computation.6 | async-start | bytes 2162688 | tf_op jit(solution)/shard_map/all_gather | solution.py:49
  60.4 376.2 %reduce-scatter.2.cloned.1.call-start = ((), (), s32[]{:S(2)}) async-start(), calls=%async_computation.5 | async-start | bytes 2162688 | tf_op jit(solution)/shard_map/reduce_scatter | solution.py:48
  160.3 276.2 %copy-start.1 = (s32[8,256]{1,0:T(8,128)S(1)}, s32[8,256]{1,0:T(8,128)}, u32[]{:S(2)}) copy-start(s32[8,256]{1,0:T(8,128)} %param.11) | copy-start | bytes 24580
  160.3 278.9 %copy-start = (f32[2,8,8,128]{3,2,1,0:T(8,128)S(1)}, f32[2,8,8,128]{3,2,1,0:T(8,128)}, u32[]{:S(2)}) copy-start(f32[2,8,8,128]{3,2,1,0:T(8,128)} %param.10) | copy-start | bytes 196612
Sparse Core Ops, SparseCore 0:
  9.2 25.9 all-gather.5
  36.9 22.7 all-gather.9
  61.5 37.6 all-gather.7
  100.9 39.1 all-gather.11
  142.4 75.6 all-gather.13
  221.7 214.7 reduce-scatter.1
where the time goes:
time: 448 us; the launch traced here: 447 us
  waiting for transfers between devices  409 us (91%)
  matrix products  18.7 us (4%)
  between operations  14.2 us (3%)
  other arithmetic  4.94 us (1%)
    reduce_scatter x1, waiting for transfers between devices, on_device(): lax.psum_scatter(collision, 'hist', scatter_dimension=2, tiled=True)  218 us
    all_gather x1, waiting for transfers between devices, on_device(): row_full = lax.all_gather(current_row, 'hist', axis=2, tiled=True)  57.7 us
    all_gather x1, waiting for transfers between devices, on_device(): lax.all_gather(greater_full, 'orow', axis=2, tiled=True)  40.8 us
    all_gather x1, waiting for transfers between devices, on_device(): lax.all_gather(lesser_full, 'orow', axis=3, tiled=True)  38.1 us
    all_gather x1, waiting for transfers between devices, on_device(): lax.all_gather(lesser_hist, 'ocol', axis=2, tiled=True)  27.1 us
    all_gather x1, waiting for transfers between devices, on_device(): lax.all_gather(greater_hist, 'ocol', axis=3, tiled=True)  24.6 us
    dot_general x1, matrix products, on_device(): jnp.einsum('csik,dstkj->cdtij', sigma_w, advanced_hist, precision=lax.Pre...  16 us
  transfers between devices with their start and end apart: 6, of which 6 were waited for; matrix products, arithmetic and copies ran while one was open for 5% of the time, Pallas kernels for 0%

commit v1 on v0

--- a/solution.py
+++ b/solution.py
@@ -26,34 +26,26 @@
     weights = jnp.where(
         slot_ids <= step_index[0], weight_table.astype(jnp.float32) / 24.0, jnp.float32(0.0)
     )
-    lesser_full, greater_full = (
-        lax.all_gather(lesser_hist, "ocol", axis=2, tiled=True),
-        lax.all_gather(greater_hist, "ocol", axis=3, tiled=True),
-    )
-    lesser_full, greater_full = (
-        lax.all_gather(lesser_full, "orow", axis=3, tiled=True),
-        lax.all_gather(greater_full, "orow", axis=2, tiled=True),
-    )
-    sigma = self_energy(lesser_full, jnp.swapaxes(greater_full, 2, 3))
-    sigma_w = sigma * weights[None, :, None, None]
+    sigma = self_energy(lesser_hist, jnp.swapaxes(greater_hist, 2, 3))
+    sigma = sigma * weights[None, :, None, None]
+    sigma = lax.all_gather(sigma, "ocol", axis=2, tiled=True)
+    sigma = lax.all_gather(sigma, "orow", axis=3, tiled=True)
     combos = jnp.einsum(
         "csik,dstkj->cdtij",
-        sigma_w,
+        sigma,
         advanced_hist,
+        precision=lax.Precision.HIGH,
+        preferred_element_type=jnp.float32,
+    )
+    collision = jnp.stack([combos[0, 0] - combos[1, 1], combos[0, 1] + combos[1, 0]])
+    hop = jnp.einsum(
+        "ki,ctkj->ctij",
+        -hopping * adjacency.astype(jnp.float32),
+        current_row,
         precision=lax.Precision.HIGHEST,
         preferred_element_type=jnp.float32,
     )
-    collision = jnp.stack([combos[0, 0] - combos[1, 1], combos[0, 1] + combos[1, 0]])
-    hop_local = -hopping * adjacency.astype(jnp.float32)
-    summed = lax.psum_scatter(collision, "hist", scatter_dimension=2, tiled=True)
-    row_full = lax.all_gather(current_row, "hist", axis=2, tiled=True)
-    summed = summed + jnp.einsum(
-        "ik,ctkj->ctij",
-        hop_local,
-        row_full,
-        precision=lax.Precision.HIGHEST,
-        preferred_element_type=jnp.float32,
-    )
+    summed = lax.psum_scatter(collision + hop, "hist", scatter_dimension=2, tiled=True)
     return jnp.stack(
         [current_row[0] + time_step * summed[1], current_row[1] - time_step * summed[0]]
     )

time: 448 us -> 315 us (0.70)
  waiting for transfers between devices: 409 us -> 282 us
  matrix products: 18.7 us -> 13.4 us
    all_gather x5 -> x2, waiting for transfers between devices: 188 us -> 65.4 us  [the longest x1 39.4 us: on_device(): sigma = lax.all_gather(sigma, 'orow', axis=3, tiled=True)]
    dot_general x2, matrix products: 18.7 us -> 13.4 us  [the longest x1 10 us: on_device(): jnp.einsum('csik,dstkj->cdtij', sigma, advanced_hist, precision=lax.Preci...]
  transfers between devices with their start and end apart: 6 -> 3, of which waited for: 6 -> 3; matrix products, arithmetic and copies ran while one was open for 5% -> 0% of each run, Pallas kernels for 0% -> 0%
where the time goes in v1:
time: 315 us; the launch traced here: 314 us
  waiting for transfers between devices  282 us (90%)
  between operations  13.8 us (4%)
  matrix products  13.4 us (4%)
  other arithmetic  4.26 us (1%)
    reduce_scatter x1, waiting for transfers between devices, on_device(): lax.psum_scatter(collision + hop, 'hist', scatter_dimension=2, tiled=True)  216 us
    all_gather x1, waiting for transfers between devices, on_device(): sigma = lax.all_gather(sigma, 'orow', axis=3, tiled=True)  39.4 us
    all_gather x1, waiting for transfers between devices, on_device(): sigma = lax.all_gather(sigma, 'ocol', axis=2, tiled=True)  26 us
    dot_general x1, matrix products, on_device(): jnp.einsum('csik,dstkj->cdtij', sigma, advanced_hist, precision=lax.Preci...  10 us
  transfers between devices with their start and end apart: 3, of which 3 were waited for; matrix products, arithmetic and copies ran while one was open for 0% of the time, Pallas kernels for 0%

profile of v1, /device:TPU:32, one launch (start us, length us, event | category | flops | bytes accessed | tf_op | source)
XLA Modules:
  0.0 314.0 jit_solution(3104474410088262736)
XLA Ops:
  6.5 0.0 all-gather.3.cloned.1.call-start
  7.2 1.2 subtract_multiply_fusion
  8.3 0.7 compare_select_fusion
  9.0 0.8 maximum_multiply_fusion
  9.8 0.0 all-gather.3.cloned.1.call-update
  9.8 0.0 all-gather.5.cloned.1.call-start
  9.9 26.0 %all-gather.3.cloned.1.call-done = f32[2,4,256,128]{3,2,1,0:T(8,128)} async-done(((f32[2,4,64,128]{3,2,1,0:T(8,128)}), f32[2,4,256,128]{3,2,1,0:T(8,128)}) %all-gather.3.cloned.1.call-update) | async-done | bytes 1048592 | tf_op jit(solution)/shard_map/all_gather | solution.py:31
  35.9 0.0 all-gather.5.cloned.1.call-update
  35.9 0.0 reduce-scatter.2.cloned.1.call-start
  36.0 39.4 %all-gather.5.cloned.1.call-done = f32[2,4,256,256]{3,2,1,0:T(8,128)} async-done(((f32[2,4,256,128]{3,2,1,0:T(8,128)}), f32[2,4,256,256]{3,2,1,0:T(8,128)}) %all-gather.5.cloned.1.call-update) | async-done | bytes 2097168 | tf_op jit(solution)/shard_map/all_gather | solution.py:32
  75.4 10.0 %fusion.3 = f32[2,2,8,256,128]{4,3,2,1,0:T(8,128)S(1)} fusion(f32[2,4,8,256,128]{4,3,2,1,0:T(8,128)} %param.9, f32[2,4,256,256]{3,2,1,0:T(8,128)} %all-gather.5.cloned.1.call-done), kind=kOutput, calls=%fused_computation.3 | convolution fusion | flops 6442450944 | bytes 14680064 | tf_op jit(solution)/shard_map/csik,dstkj->cdtij/dot_general | solution.py:33
  85.4 0.0 copy-start
  85.4 0.0 copy-start.1
  85.4 0.2 fusion.8
  85.7 0.6 copy-done
  86.2 0.0 copy-done.1
  86.2 3.3 %maximum_add_fusion = f32[2,8,256,128]{3,2,1,0:T(8,128)} fusion(f32[1,8,256,128]{3,2,1,0:T(8,128)S(1)} %get-tuple-element.6, f32[1,8,256,128]{3,2,1,0:T(8,128)S(1)} %get-tuple-element.5, f32[2,8,8,128]{3,2,1,0:T(8,128)S(1)} %copy-done, s32[8,256]{1,0:T(8,128)S(1)} %copy-done.1), kind=kOutput, calls=%fused_computation.4 | convolution fusion | flops 51384320 | bytes 4268032 | tf_op jit(solution)/shard_map/ki,ctkj->ctij/dot_general | solution.py:41
  89.6 0.0 reduce-scatter.2.cloned.1.call-update
  89.6 216.4 %reduce-scatter.2.cloned.1.call-done = f32[2,8,8,128]{3,2,1,0:T(8,128)} async-done(((f32[2,8,256,128]{3,2,1,0:T(8,128)}), f32[2,8,8,128]{3,2,1,0:T(8,128)}) %reduce-scatter.2.cloned.1.call-update) | async-done | bytes 65552 | tf_op jit(solution)/shard_map/reduce_scatter | solution.py:48
  306.0 0.8 fusion.10
  306.8 0.6 pad_maximum_fusion
Async XLA Ops:
  6.5 29.4 %all-gather.3.cloned.1.call-start = ((), (), s32[]{:S(2)}) async-start(), calls=%async_computation.1 | async-start | bytes 1310720 | tf_op jit(solution)/shard_map/all_gather | solution.py:31
  9.8 65.5 %all-gather.5.cloned.1.call-start = ((), (), s32[]{:S(2)}) async-start(), calls=%async_computation.2 | async-start | bytes 3145728 | tf_op jit(solution)/shard_map/all_gather | solution.py:32
  35.9 270.1 %reduce-scatter.2.cloned.1.call-start = ((), (), s32[]{:S(2)}) async-start(), calls=%async_computation.3 | async-start | bytes 2162688 | tf_op jit(solution)/shard_map/reduce_scatter | solution.py:48
  85.4 0.8 copy-start
  85.4 0.8 copy-start.1
Sparse Core Ops, SparseCore 0:
  10.0 25.9 all-gather.2
  37.7 37.6 all-gather.4
  89.7 216.2 reduce-scatter.1

commit v2 on v1

v2 whole, which is shorter than its diff:
```python
import functools

import jax
import jax.numpy as jnp
from jax import lax
from jax.experimental import pallas as pl
from jax.experimental.pallas import tpu as pltpu
from jax.sharding import PartitionSpec as P

coupling_square = 0.25
hopping = 4.0
time_step = 0.01

NZ, NY = 8, 4
NS, NT = 4, 8
ROWS, COLS = 64, 128
HALVES = 2
RB = ROWS // HALVES
NZZ = NZ // HALVES
STAGES = ((0, 0, 4), (0, 4, 4), (1, 0, 4), (1, 4, 4))
MESH = pl.DeviceIdType.MESH
f32, bf16 = jnp.float32, jnp.bfloat16


def split(x):
    hi = x.astype(bf16)
    return hi, (x - hi.astype(f32)).astype(bf16)


def kernel(
    table, step, lesser, greater, advanced, row, adjacency, out,
    les_b, gre_b, adv_b, row_b, adj_b, gath, lhs_hi, lhs_lo, rhs_hi, rhs_lo, hop_l, hop_r,
    in_sem, adv_sem, gs, gr, ys, yr, zs, zr, *bufs,
):
    n_st = len(STAGES)
    part, y1, y2, zb = (bufs[i * n_st : (i + 1) * n_st] for i in range(4))
    h, r, c = (lax.axis_index(a) for a in ("hist", "orow", "ocol"))
    z, y = lax.div(h, NY), lax.rem(h, NY)
    x, k = lax.div(c, 2) * 2 + r, lax.rem(c, 2)

    def wrap(v, n):
        return lax.rem(v + n, n)

    def dev(dx=0, dy=0, dz=0, other=False):
        xx = wrap(x + dx, 4)
        kk = 1 - k if other else k
        hh = wrap(z + dz, NZ) * NY + wrap(y + dy, NY)
        return (hh, lax.rem(xx, 2), lax.div(xx, 2) * 2 + kk)

    def remote(src, dst, ss, rs, to):
        return pltpu.make_async_remote_copy(
            src_ref=src, dst_ref=dst, send_sem=ss, recv_sem=rs, device_id=to, device_id_type=MESH
        )

    inputs = [
        pltpu.make_async_copy(a, b, in_sem.at[i])
        for i, (a, b) in enumerate(
            ((lesser, les_b), (greater, gre_b), (row, row_b), (adjacency, adj_b))
        )
    ]
    for copy in inputs:
        copy.start()
    adv = [pltpu.make_async_copy(advanced.at[:, :, t], adv_b.at[t], adv_sem.at[t]) for t in range(NT)]
    for copy in adv:
        copy.start()

    barrier = pltpu.get_barrier_semaphore()
    friends = [dev(dx=1), dev(dx=-1), dev(other=True), dev(dy=1), dev(dy=-1)]
    friends += [dev(dz=d) for d in range(1, NZ)]
    for friend in friends:
        pl.semaphore_signal(barrier, inc=1, device_id=friend, device_id_type=MESH)

    inputs[0].wait()
    inputs[1].wait()
    for s in range(NS):
        used = h * NS + s <= step[0]
        scale = jnp.where(used, table[s], 0).astype(f32) * (coupling_square / 24.0)
        lr, li = les_b[0, s], les_b[1, s]
        gre, gim = gre_b[0, s].T, gre_b[1, s].T
        sr = (lr * lr - li * li) * scale
        si = (2.0 * lr * li) * scale
        re = sr * gre - si * gim
        im = sr * gim + si * gre
        for hf in range(HALVES):
            gath[hf, 0, s, 0] = re[hf * RB : (hf + 1) * RB]
            gath[hf, 0, s, 1] = im[hf * RB : (hf + 1) * RB]

    pl.semaphore_wait(barrier, len(friends))

    slot_of = {0: (0, False), 1: (0, True), 2: (-1, False), 3: (-1, True),
               4: (1, False), 5: (1, True), 6: (2, False), 7: (2, True)}
    lo_s, hi_s, all_s = pl.ds(0, 2), pl.ds(2, 2), pl.ds(0, 4)

    def piece(hf, n, src_slot, dst_slot, ss, to):
        return remote(
            gath.at[hf, src_slot, ss], gath.at[hf, dst_slot, ss], gs.at[hf, n], gr.at[hf, n], to
        )

    right, left, twin = dev(dx=1), dev(dx=-1), dev(other=True)
    g = [
        [
            piece(hf, 0, 0, 2, lo_s, right),
            piece(hf, 1, 0, 4, hi_s, left),
            piece(hf, 2, 0, 2, hi_s, right),
            piece(hf, 3, 0, 4, lo_s, left),
            piece(hf, 4, 0, 1, all_s, twin),
            piece(hf, 5, 2, 6, lo_s, right),
            piece(hf, 6, 4, 6, hi_s, left),
            piece(hf, 7, 2, 3, lo_s, twin),
            piece(hf, 8, 4, 5, hi_s, twin),
            piece(hf, 9, 2, 3, hi_s, twin),
            piece(hf, 10, 4, 5, lo_s, twin),
            piece(hf, 11, 6, 7, lo_s, twin),
            piece(hf, 12, 6, 7, hi_s, twin),
        ]
        for hf in range(HALVES)
    ]

    def to_lhs(hf, slot, s_range):
        dx, other = slot_of[slot]
        xx = wrap(x + dx, 4)
        kh = dx % 2
        block = lax.div(xx, 2) * 2 + (1 - k if other else k)
        for s in s_range:
            for cc in range(2):
                hi, lo = split(gath[hf, slot, s, cc])
                lhs_hi[hf, kh, s, cc, block] = hi
                lhs_lo[hf, kh, s, cc, block] = lo

    def begin(hf, names):
        for n in names:
            g[hf][n].start()

    def arrived(hf, names):
        for n in names:
            g[hf][n].wait_recv()

    def to_rhs(first, count):
        def one(t, carry):
            for s in range(NS):
                for cc in range(2):
                    for kh in range(2):
                        half = wrap(r + kh, 2)
                        rows = pl.ds(pl.multiple_of(half * 128, 128), 128)
                        hi, lo = split(adv_b[t, cc, s, rows, :])
                        rhs_hi[t, s, kh * 128 : (kh + 1) * 128, cc * 128 : (cc + 1) * 128] = hi
                        rhs_lo[t, s, kh * 128 : (kh + 1) * 128, cc * 128 : (cc + 1) * 128] = lo
            return carry

        for t in range(first, first + count):
            adv[t].wait()
        lax.fori_loop(first, first + count, one, 0)

    begin(0, (0, 1, 2, 3, 4))
    if HALVES > 1:
        begin(1, (0, 1))

    inputs[2].wait()
    inputs[3].wait()
    adj = adj_b[...].astype(f32) * -hopping
    adj_t = jnp.concatenate([adj, adj, jnp.zeros((112, 256), f32)], axis=0).T.astype(bf16)
    for hf in range(HALVES):
        for b in range(4):
            first = b * ROWS + hf * RB
            hop_l[hf, b * RB : (b + 1) * RB, :] = adj_t[first : first + RB]
    for t in range(NT):
        both = jnp.concatenate([row_b[0, t], row_b[1, t]], axis=1)
        hi = both.astype(bf16).astype(f32)
        full = jnp.concatenate([hi, both - hi, jnp.zeros((112, 256), f32)], axis=0)
        hop_r[t] = full.astype(bf16)

    to_lhs(0, 0, range(NS))
    to_rhs(0, 4)

    def gather_rest(hf, step_n):
        if step_n == 0:
            arrived(hf, (0, 1))
            begin(hf, (5, 6, 7, 8))
        elif step_n == 1:
            arrived(hf, (2, 3))
            begin(hf, (9, 10))
            to_lhs(hf, 2, range(NS))
            to_lhs(hf, 4, range(NS))
            arrived(hf, (4,))
            to_lhs(hf, 1, range(NS))
        elif step_n == 2:
            arrived(hf, (5, 6))
            begin(hf, (11, 12))
            to_lhs(hf, 6, range(NS))
            arrived(hf, (7, 8, 9, 10))
            to_lhs(hf, 3, range(NS))
            to_lhs(hf, 5, range(NS))
        else:
            arrived(hf, (11, 12))
            to_lhs(hf, 7, range(NS))

    gather_rest(0, 0)
    if HALVES > 1:
        begin(1, (2, 3, 4))
        to_lhs(1, 0, range(NS))
    to_rhs(4, 4)
    gather_rest(0, 1)
    if HALVES > 1:
        gather_rest(1, 0)
    gather_rest(0, 2)
    gather_rest(0, 3)

    half = NZZ // 2
    first_h, second_h = pl.ds(0, half), pl.ds(half, half)

    def y_copies(st):
        p = part[st]
        up, down = dev(dy=1), dev(dy=-1)
        ring = [
            (p.at[wrap(y + 2, NY), first_h], y1[st].at[0], up),
            (p.at[wrap(y + 2, NY), second_h], y1[st].at[1], down),
            (p.at[wrap(y + 1, NY), second_h], y2[st].at[0, second_h], up),
            (p.at[wrap(y - 1, NY), first_h], y2[st].at[1, first_h], down),
            (p.at[wrap(y + 1, NY), first_h], y2[st].at[0, first_h], up),
            (p.at[wrap(y - 1, NY), second_h], y2[st].at[1, second_h], down),
        ]
        return [remote(a, b, ys.at[st, i], yr.at[st, i], to) for i, (a, b, to) in enumerate(ring)]

    def z_copy(st, d):
        zz = lax.div(wrap(z + d, NZ), HALVES)
        return remote(part[st].at[y, zz], zb[st].at[d - 1], zs.at[st, d - 1], zr.at[st, d - 1], dev(dz=d))

    def z_each(st, act):
        hf = STAGES[st][0]
        for d in range(1, NZ):
            if HALVES == 1:
                act(z_copy(st, d))
            else:
                @pl.when(lax.rem(z + d, HALVES) == hf)
                def _():
                    act(z_copy(st, d))

    def compute(st):
        hf, t0, nt = STAGES[st]

        def one(t, carry):
            tt = t0 + t
            acc = None
            for s in range(NS):
                def left_of(ref):
                    a = [ref[hf, kh, s].reshape(8 * RB, 128) for kh in range(2)]
                    return jnp.concatenate(a, axis=1)

                a_hi, a_lo = left_of(lhs_hi), left_of(lhs_lo)
                b_hi, b_lo = rhs_hi[tt, s], rhs_lo[tt, s]
                for a, b in ((a_hi, b_hi), (a_hi, b_lo), (a_lo, b_hi)):
                    term = jnp.dot(a, b, preferred_element_type=f32)
                    acc = term if acc is None else acc + term
            hop = jnp.dot(hop_l[hf], hop_r[tt], preferred_element_type=f32)
            m = 4 * RB
            re = acc[:m, :128] - acc[m:, 128:] + hop[:, :128]
            im = acc[:m, 128:] + acc[m:, :128] + hop[:, 128:]
            re, im = (v.reshape(NZZ, NY, 8, 128) for v in (re, im))
            for yy in range(NY):
                part[st][yy, :, 0, t] = re[:, yy]
                part[st][yy, :, 1, t] = im[:, yy]
            return carry

        lax.fori_loop(0, nt, one, 0)
        for copy in y_copies(st)[:4]:
            copy.start()

    def y_late(st):
        copies = y_copies(st)
        copies[0].wait_recv()
        up = wrap(y + 1, NY)
        part[st][up, :half] = part[st][up, :half] + y1[st][0]
        copies[4].start()
        copies[1].wait_recv()
        down = wrap(y - 1, NY)
        part[st][down, half:] = part[st][down, half:] + y1[st][1]
        copies[5].start()

    def z_send(st):
        for copy in y_copies(st)[2:]:
            copy.wait_recv()
        part[st][y] = part[st][y] + y2[st][0] + y2[st][1]
        z_each(st, lambda copy: copy.start())

    def finish(st):
        hf, t0, nt = STAGES[st]

        def receive():
            total = part[st][y, lax.div(z, HALVES)]
            for d in range(1, NZ):
                z_copy(st, d).wait_recv()
                total = total + zb[st][d - 1]
            out[0, t0 : t0 + nt] = row_b[0, t0 : t0 + nt] + time_step * total[1]
            out[1, t0 : t0 + nt] = row_b[1, t0 : t0 + nt] - time_step * total[0]

        if HALVES == 1:
            receive()
        else:
            pl.when(lax.rem(z, HALVES) == hf)(receive)

    compute(0)
    gather_rest(1, 1)
    compute(1)
    y_late(0)
    gather_rest(1, 2)
    gather_rest(1, 3)
    compute(2)
    y_late(1)
    z_send(0)
    compute(3)
    y_late(2)
    z_send(1)
    y_late(3)
    finish(0)
    z_send(2)
    finish(1)
    z_send(3)
    finish(2)
    finish(3)

    for hf in range(HALVES):
        for copy in g[hf]:
            copy.wait_send()
    for st in range(n_st):
        for copy in y_copies(st):
            copy.wait_send()
        z_each(st, lambda copy: copy.wait_send())


def on_device(
    lesser_hist, greater_hist, advanced_hist, current_row, adjacency, weight_table, step_index
):
    vmem, dma = pltpu.VMEM, pltpu.SemaphoreType.DMA
    n_st = len(STAGES)
    scratch = [
        vmem((2, NS, ROWS, COLS), f32),
        vmem((2, NS, COLS, ROWS), f32),
        vmem((NT, 2, NS, 256, COLS), f32),
        vmem((2, NT, 8, COLS), f32),
        vmem((8, 256), jnp.int32),
        vmem((HALVES, 8, NS, 2, RB, COLS), f32),
        vmem((HALVES, 2, NS, 2, 4, RB, COLS), bf16),
        vmem((HALVES, 2, NS, 2, 4, RB, COLS), bf16),
        vmem((NT, NS, 256, 256), bf16),
        vmem((NT, NS, 256, 256), bf16),
        vmem((HALVES, 4 * RB, 128), bf16),
        vmem((NT, 128, 256), bf16),
        dma((4,)), dma((NT,)),
        dma((HALVES, 13)), dma((HALVES, 13)),
        dma((n_st, 6)), dma((n_st, 6)),
        dma((n_st, NZ - 1)), dma((n_st, NZ - 1)),
    ]
    scratch += [vmem((NY, NZZ, 2, nt, 8, COLS), f32) for _, _, nt in STAGES]
    scratch += [vmem((2, NZZ // 2, 2, nt, 8, COLS), f32) for _, _, nt in STAGES]
    scratch += [vmem((2, NZZ, 2, nt, 8, COLS), f32) for _, _, nt in STAGES]
    scratch += [vmem((NZ - 1, 2, nt, 8, COLS), f32) for _, _, nt in STAGES]
    smem = pl.BlockSpec(memory_space=pltpu.SMEM)
    anywhere = pl.BlockSpec(memory_space=pl.ANY)
    return pl.pallas_call(
        kernel,
        out_shape=jax.ShapeDtypeStruct((2, NT, 8, COLS), f32),
        in_specs=[smem, smem] + [anywhere] * 5,
        out_specs=pl.BlockSpec(memory_space=vmem),
        scratch_shapes=scratch,
        compiler_params=pltpu.CompilerParams(
            collective_id=0, has_side_effects=True, vmem_limit_bytes=56 * 1024 * 1024
        ),
        name="row_step",
    )(weight_table, step_index, lesser_hist, greater_hist, advanced_hist, current_row, adjacency)


def solution(mesh):
    in_specs = (
        P(None, "hist", "ocol", "orow"),
        P(None, "hist", "orow", "ocol"),
        P(None, "hist", "ocol", None, "orow"),
        P(None, "ocol", "hist", "orow"),
        P("hist", None),
        P("hist"),
        P(),
    )
    out_specs = P(None, "ocol", "hist", "orow")
    return jax.shard_map(
        on_device, mesh=mesh, in_specs=in_specs, out_specs=out_specs, check_vma=False
    )
```

time: 315 us -> 57.1 us (0.18)
  waiting for transfers between devices: 282 us -> 0 us
  Pallas kernels: 0 us -> 52.9 us
  matrix products: 13.4 us -> 0 us
  between operations: 13.8 us -> 0.66 us
  other arithmetic: 4.26 us -> 0 us
    reduce_scatter x1 -> x0, waiting for transfers between devices: 216 us -> none  [on_device(): lax.psum_scatter(collision + hop, 'hist', scatter_dimension=2, tiled=True)]
    all_gather x2 -> x0, waiting for transfers between devices: 65.4 us -> none  [the longest x1 39.4 us: on_device(): sigma = lax.all_gather(sigma, 'orow', axis=3, tiled=True)]
    pallas_call x0 -> x1, Pallas kernels: none -> 52.9 us  [on_device(): pl.pallas_call(kernel, out_shape=jax.ShapeDtypeStruct((2, NT, 8, COLS), f...]
    dot_general x2 -> x0, matrix products: 13.4 us -> none  [the longest x1 10 us: on_device(): jnp.einsum('csik,dstkj->cdtij', sigma, advanced_hist, precision=lax.Preci...]
  transfers between devices with their start and end apart: 3 -> 0, of which waited for: 3 -> 0; matrix products, arithmetic and copies ran while one was open for 0% -> 0% of each run, Pallas kernels for 0% -> 0%
where the time goes in v2:
time: 57.1 us; the launch traced here: 57 us
  Pallas kernels  52.9 us (93%)
  local copies, waits for them, and re-layouts  3.42 us (6%)
  between operations  0.66 us (1%)
    pallas_call x1, Pallas kernels, on_device(): pl.pallas_call(kernel, out_shape=jax.ShapeDtypeStruct((2, NT, 8, COLS), f...  52.9 us
    unnamed x2, local copies, waits for them, and re-layouts  3.42 us

profile of v2, /device:TPU:32, one launch (start us, length us, event | category | flops | bytes accessed | tf_op | source)
XLA Modules:
  0.0 57.0 jit_solution(9739478973466014471)
XLA Ops:
  0.7 1.9 %copy.8.greater = f32[2,4,128,64]{3,2,1,0:T(8,128)} copy(f32[2,4,128,64]{2,3,1,0:T(8,128)} %param.8) | data formatting | bytes 524288 | tf_op args[1]
  2.6 52.9 %row_step.1 = f32[2,8,8,128]{3,2,1,0:T(8,128)} custom-call(s32[4]{0:T(128)} %table.1, s32[1]{0:T(128)S(6)} %copy.10.step, f32[2,4,64,128]{3,2,1,0:T(8,128)} %lesser.1, f32[2,4,128,64]{3,2,1,0:T(8,128)} %copy.8.greater, f32[2,4,8,256,128]{4,3,2,1,0:T(8,128)} %advanced.1, f32[2,8,8,128]{3,2,1,0:T(8,128)} %row.1, s32[8,256]{1,0:T(8,128)} %adjacency.1), custom_call_target="tpu_custom_call" | custom-call | tf_op jit(solution)/shard_map/row_step/pallas_call | solution.py:359
  55.5 1.5 %copy.11 = f32[2,8,8,128]{3,2,1,0:T(8,128)} copy(f32[2,8,8,128]{3,2,1,0:T(8,128)} %row_step.1) | data formatting | bytes 131072

commit v3 on v1

v3 whole, which is shorter than its diff:
```python
import jax
import jax.numpy as jnp
from jax import lax
from jax.experimental import pallas as pl
from jax.experimental.pallas import tpu as pltpu
from jax.sharding import PartitionSpec as P

coupling_square = 0.25
hopping = 4.0
time_step = 0.01

NZ, NY = 8, 4
NS, NT = 4, 8
ROWS, COLS = 64, 128
HALVES = 2
STAGES = (("D", 0, 0, 2), ("A", 0, 2, 4), ("B", 0, 6, 2), ("B", 1, 0, 4), ("B", 1, 4, 4))
G = -1
PLAN = (0, 1, 2, G, G, G, 3, 4, 1, 0, 2, 1, 3, 2, 0, 4, 1, 3, 4, 1, 2, 1, 3, 4)
MESH = pl.DeviceIdType.MESH
f32, bf16 = jnp.float32, jnp.bfloat16


def split(x):
    hi = x.astype(bf16)
    return hi, (x - hi.astype(f32)).astype(bf16)


def upper(shape):
    return lax.broadcasted_iota(jnp.int32, shape, len(shape) - 2) % 8 < 4


def swapped(x):
    tiles = x.reshape(x.shape[0] // 8, 8, x.shape[1])
    return pltpu.roll(tiles, 4, 1).reshape(x.shape)


def kernel(
    table_h, step_h, lesser, greater, advanced, row, adjacency, out,
    table, step, les_b, gre_b, adv_b, row_b, adj_b, gath, lhs_hi, lhs_lo, rhs_hi, rhs_lo, hop_l, hop_r,
    in_sem, adv_sem, gs, gr, *bufs,
):
    h, r, c = (lax.axis_index(a) for a in ("hist", "orow", "ocol"))
    z, y = lax.div(h, NY), lax.rem(h, NY)
    x, k = lax.div(c, 2) * 2 + r, lax.rem(c, 2)

    def wrap(v, n):
        return lax.rem(v + n, n)

    def dev(dx=0, dy=0, dz=0, other=False):
        xx = wrap(x + dx, 4)
        kk = 1 - k if other else k
        hh = wrap(z + dz, NZ) * NY + wrap(y + dy, NY)
        return (hh, lax.rem(xx, 2), lax.div(xx, 2) * 2 + kk)

    def remote(src, dst, ss, rs, to):
        return pltpu.make_async_remote_copy(
            src_ref=src, dst_ref=dst, send_sem=ss, recv_sem=rs, device_id=to, device_id_type=MESH
        )

    inputs = [
        pltpu.make_async_copy(a, b, in_sem.at[i])
        for i, (a, b) in enumerate(
            ((table_h, table), (step_h, step), (lesser, les_b), (greater, gre_b), (row, row_b), (adjacency, adj_b))
        )
    ]
    for copy in inputs:
        copy.start()
    adv = [pltpu.make_async_copy(advanced.at[:, :, t], adv_b.at[t], adv_sem.at[t]) for t in range(NT)]
    for copy in adv:
        copy.start()

    barrier = pltpu.get_barrier_semaphore()
    friends = [dev(dx=1), dev(dx=-1), dev(other=True), dev(dy=1), dev(dy=-1), dev(dy=2)]
    friends += [dev(dz=d) for d in range(1, NZ)]
    for friend in friends:
        pl.semaphore_signal(barrier, inc=1, device_id=friend, device_id_type=MESH)

    for copy in inputs[:4]:
        copy.wait()
    above = upper((ROWS, COLS))
    for s in range(NS):
        used = h * NS + s <= step[0]
        scale = jnp.where(used, table[s], 0).astype(f32) * (coupling_square / 24.0)
        lr, li = les_b[0, s], les_b[1, s]
        gre, gim = gre_b[0, s], gre_b[1, s]
        sr = (lr * lr - li * li) * scale
        si = (2.0 * lr * li) * scale
        re = sr * gre - si * gim
        im = sr * gim + si * gre
        gath[0, 0, s] = jnp.where(above, re, swapped(im))
        gath[1, 0, s] = jnp.where(above, swapped(re), im)

    pl.semaphore_wait(barrier, len(friends))

    slot_of = {0: (0, False), 1: (0, True), 2: (-1, False), 3: (-1, True),
               4: (1, False), 5: (1, True), 6: (2, False), 7: (2, True)}
    lo_s, hi_s, all_s = pl.ds(0, 2), pl.ds(2, 2), pl.ds(0, 4)
    right, left, twin = dev(dx=1), dev(dx=-1), dev(other=True)
    pieces = (
        (0, 2, lo_s, right), (0, 4, hi_s, left), (0, 2, hi_s, right), (0, 4, lo_s, left), (0, 1, all_s, twin),
        (2, 6, lo_s, right), (4, 6, hi_s, left),
        (2, 3, lo_s, twin), (4, 5, hi_s, twin), (2, 3, hi_s, twin), (4, 5, lo_s, twin),
        (6, 7, lo_s, twin), (6, 7, hi_s, twin),
    )

    def piece(hf, n):
        a, b, ss, to = pieces[n]
        return remote(gath.at[hf, a, ss], gath.at[hf, b, ss], gs.at[hf, n], gr.at[hf, n], to)

    def to_lhs(hf, slot, s_range=range(NS)):
        dx, other = slot_of[slot]
        xx = wrap(x + dx, 4)
        kh = dx % 2
        block = lax.div(xx, 2) * 2 + (1 - k if other else k)
        for s in s_range:
            v = gath[hf, slot, s]
            turned = swapped(v)
            for cc, part_v in enumerate((v, jnp.where(above, -turned, turned))):
                hi, lo = split(part_v)
                lhs_hi[hf, s, cc, kh, block] = hi
                lhs_lo[hf, s, cc, kh, block] = lo

    def begin(hf, names):
        for n in names:
            piece(hf, n).start()

    def arrived(hf, names):
        for n in names:
            piece(hf, n).wait_recv()

    def to_rhs(first, count):
        def one(pair, carry):
            for t in range(2):
                for s in range(NS):
                    for cc in range(2):
                        for kh in range(2):
                            rows = pl.ds(pl.multiple_of(wrap(r + kh, 2) * 128, 128), 128)
                            hi, lo = split(adv_b[2 * pair + t, cc, s, rows, :])
                            at = cc * 256 + kh * 128
                            rhs_hi[pair, s, at : at + 128, t * 128 : (t + 1) * 128] = hi
                            rhs_lo[pair, s, at : at + 128, t * 128 : (t + 1) * 128] = lo
            return carry

        for t in range(2 * first, 2 * (first + count)):
            adv[t].wait()
        lax.fori_loop(first, first + count, one, 0)

    begin(0, (0, 1, 2, 3, 4))
    begin(1, (0, 1))

    inputs[4].wait()
    inputs[5].wait()
    adj = adj_b[...].astype(f32) * -hopping
    adj_t = jnp.concatenate([adj, adj, adj, adj, jnp.zeros((96, 256), f32)], axis=0).T
    adj_s = swapped(adj_t)
    top = upper((256, 128))
    lane = lax.broadcasted_iota(jnp.int32, (256, 128), 1)
    keep = top == (lane < 16)
    hop_l[0] = jnp.where(keep, jnp.where(top, adj_t, adj_s), 0.0).astype(bf16)
    hop_l[1] = jnp.where(keep, jnp.where(top, adj_s, adj_t), 0.0).astype(bf16)
    for pair in range(NT // 2):
        rows = []
        for cc in range(2):
            v = jnp.concatenate([row_b[cc, 2 * pair], row_b[cc, 2 * pair + 1]], axis=1)
            hi = v.astype(bf16).astype(f32)
            rows += [hi, v - hi]
        rows.append(jnp.zeros((96, 256), f32))
        hop_r[pair] = jnp.concatenate(rows, axis=0).astype(bf16)

    to_lhs(0, 0)
    to_rhs(0, 2)

    def gather_rest(hf, step_n):
        if step_n == 0:
            arrived(hf, (0, 1))
            begin(hf, (5, 6, 7, 8))
        elif step_n == 1:
            arrived(hf, (2, 3))
            begin(hf, (9, 10))
            to_lhs(hf, 2)
            to_lhs(hf, 4)
            arrived(hf, (4,))
            to_lhs(hf, 1)
        elif step_n == 2:
            arrived(hf, (5, 6))
            begin(hf, (11, 12))
            to_lhs(hf, 6)
            arrived(hf, (7, 8, 9, 10))
            to_lhs(hf, 3)
            to_lhs(hf, 5)
        else:
            arrived(hf, (11, 12))
            to_lhs(hf, 7)

    gather_rest(0, 0)
    begin(1, (2, 3, 4))
    to_lhs(1, 0)
    to_rhs(2, 2)
    gather_rest(0, 1)
    gather_rest(1, 0)
    gather_rest(0, 2)
    gather_rest(0, 3)

    def product(st, store):
        _, hf, t0, nt = STAGES[st]

        def one(i, carry):
            pair = t0 // 2 + i
            acc = jnp.dot(hop_l[hf], hop_r[pair], preferred_element_type=f32)
            for s in range(NS):
                def left_of(ref):
                    a = [ref[hf, s, cc, kh].reshape(256, 128) for cc in range(2) for kh in range(2)]
                    return jnp.concatenate(a, axis=1)

                a_hi, a_lo = left_of(lhs_hi), left_of(lhs_lo)
                b_hi, b_lo = rhs_hi[pair, s], rhs_lo[pair, s]
                for a, b in ((a_hi, b_hi), (a_hi, b_lo), (a_lo, b_hi)):
                    acc = acc + jnp.dot(a, b, preferred_element_type=f32)
            for t in range(2):
                store(acc[:, t * 128 : (t + 1) * 128].reshape(NZ, NY, 8, 128), 2 * i + t)
            return carry

        lax.fori_loop(0, nt // 2, one, 0)

    def finish(st, total):
        _, hf, t0, nt = STAGES[st]
        total = total.reshape(nt * 8, 128)
        turned = swapped(total) * time_step
        change = jnp.where(upper(total.shape), turned, -turned).reshape(nt, 8, 128)
        rows = slice(4 * hf, 4 * hf + 4)
        for cc in range(2):
            mine = row_b[cc, t0 : t0 + nt, rows] + change[:, 4 * cc : 4 * cc + 4]
            out[cc, t0 : t0 + nt, rows] = mine

    class Stage:
        def __init__(self, st, refs):
            self.st, self.refs, self.sems = st, refs[:-2], refs[-2:]
            self.table = self.copies()
            self.steps = self.program()

        def copy(self, n):
            src, dst, to = self.table[n]()
            return remote(src, dst, self.sems[0].at[n], self.sems[1].at[n], to)

        def start(self, *names):
            for n in names:
                self.copy(n).start()

        def got(self, *names):
            for n in names:
                self.copy(n).wait_recv()

        def next(self):
            self.steps.pop(0)()

        def sent(self):
            for n in range(len(self.table)):
                self.copy(n).wait_send()

    def last_z(p, slots):
        return [
            lambda d=d: (p.at[y, wrap(z + d, NZ)], slots.at[d - 1], dev(dz=d)) for d in range(1, NZ)
        ]

    def ascending(stage, first):
        p, slots = stage.refs[0], stage.refs[-1]
        for to in range(NZ):
            @pl.when(z != to)
            def _():
                d = wrap(to - z, NZ)
                ss, rs = (s.at[first + d - 1] for s in stage.sems)
                remote(p.at[y, to], slots.at[d - 1], ss, rs, (to * NY + y, r, c)).start()

    class B(Stage):
        def copies(self):
            p, one, two, slots = self.refs
            lo, hi = pl.ds(0, NZ // 2), pl.ds(NZ // 2, NZ // 2)
            up, down = dev(dy=1), dev(dy=-1)
            y1, y2, y3 = wrap(y + 1, NY), wrap(y + 2, NY), wrap(y - 1, NY)
            return [
                lambda: (p.at[y2, lo], one.at[0], up),
                lambda: (p.at[y2, hi], one.at[1], down),
                lambda: (p.at[y1, hi], two.at[0, hi], up),
                lambda: (p.at[y3, lo], two.at[1, lo], down),
                lambda: (p.at[y1, lo], two.at[0, lo], up),
                lambda: (p.at[y3, hi], two.at[1, hi], down),
            ] + last_z(p, slots)

        def program(self):
            p, one, two, slots = self.refs

            def first():
                def store(v, t):
                    for yy in range(NY):
                        p[yy, :, t] = v[:, yy]

                product(self.st, store)
                self.start(0, 1, 2, 3)

            def late():
                n = NZ // 2
                y1, y3 = wrap(y + 1, NY), wrap(y - 1, NY)
                self.got(0)
                p[y1, :n] = p[y1, :n] + one[0]
                self.start(4)
                self.got(1)
                p[y3, n:] = p[y3, n:] + one[1]
                self.start(5)

            def send():
                self.got(2, 3, 4, 5)
                p[y] = p[y] + two[0] + two[1]
                ascending(self, 6)

            def end():
                self.got(*range(6, 6 + NZ - 1))
                total = p[y, z]
                for d in range(NZ - 1):
                    total = total + slots[d]
                finish(self.st, total)

            return [first, late, send, end]

    class D(Stage):
        def copies(self):
            p, two, slots = self.refs
            return [
                lambda d=d: (p.at[wrap(y + d, NY)], two.at[d - 1], dev(dy=d)) for d in range(1, NY)
            ] + last_z(p, slots)

        def program(self):
            p, two, slots = self.refs

            def first():
                def store(v, t):
                    for yy in range(NY):
                        p[yy, :, t] = v[:, yy]

                product(self.st, store)
                self.start(*range(NY - 1))

            def send():
                self.got(*range(NY - 1))
                p[y] = p[y] + two[0] + two[1] + two[2]
                ascending(self, NY - 1)

            def end():
                self.got(*range(NY - 1, NY + NZ - 2))
                total = p[y, z]
                for d in range(NZ - 1):
                    total = total + slots[d]
                finish(self.st, total)

            return [first, send, end]

    class A(Stage):
        def copies(self):
            p, one, two, three, four, slots = self.refs
            lo, hi = pl.ds(0, NY // 2), pl.ds(NY // 2, NY // 2)
            up, down = dev(dz=1), dev(dz=-1)

            def at(d):
                return wrap(z + d, NZ)

            return [
                lambda: (p.at[at(4), lo], one.at[0], up),
                lambda: (p.at[at(4), hi], one.at[1], down),
                lambda: (p.at[at(3), hi], two.at[0, hi], up),
                lambda: (p.at[at(-3), lo], two.at[1, lo], down),
                lambda: (p.at[at(3), lo], two.at[0, lo], up),
                lambda: (p.at[at(-3), hi], two.at[1, hi], down),
                lambda: (p.at[at(2)], three.at[0], up),
                lambda: (p.at[at(-2)], three.at[1], down),
                lambda: (p.at[at(1)], four.at[0], up),
                lambda: (p.at[at(-1)], four.at[1], down),
            ] + [
                lambda d=d: (p.at[z, wrap(y + d, NY)], slots.at[d - 1], dev(dy=d)) for d in range(1, NY)
            ]

        def program(self):
            p, one, two, three, four, slots = self.refs
            n = NY // 2

            def at(d):
                return wrap(z + d, NZ)

            def first():
                def store(v, t):
                    p[:, :, t] = v

                product(self.st, store)
                self.start(0, 1, 2, 3)

            def second():
                self.got(0)
                p[at(3), :n] = p[at(3), :n] + one[0]
                self.start(4)
                self.got(1)
                p[at(-3), n:] = p[at(-3), n:] + one[1]
                self.start(5)

            def third():
                self.got(2, 4)
                p[at(2)] = p[at(2)] + two[0]
                self.start(6)
                self.got(3, 5)
                p[at(-2)] = p[at(-2)] + two[1]
                self.start(7)

            def fourth():
                self.got(6)
                p[at(1)] = p[at(1)] + three[0]
                self.start(8)
                self.got(7)
                p[at(-1)] = p[at(-1)] + three[1]
                self.start(9)

            def send():
                self.got(8, 9)
                p[z] = p[z] + four[0] + four[1]
                self.start(10, 11, 12)

            def end():
                self.got(10, 11, 12)
                finish(self.st, p[z, y] + slots[0] + slots[1] + slots[2])

            return [first, second, third, fourth, send, end]

    stages, used_refs = [], 0
    for st, (kind, _, _, _) in enumerate(STAGES):
        count = len(stage_scratch(STAGES[st]))
        stages.append({"A": A, "B": B, "D": D}[kind](st, bufs[used_refs : used_refs + count]))
        used_refs += count
    gather_step = 1
    for name in PLAN:
        if name == G:
            gather_rest(1, gather_step)
            gather_step += 1
        else:
            stages[name].next()

    for hf in range(HALVES):
        for n in range(len(pieces)):
            piece(hf, n).wait_send()
    for stage in stages:
        stage.sent()


def stage_scratch(stage):
    kind, _, _, nt = stage
    dma = pltpu.SemaphoreType.DMA

    def block(*lead):
        return pltpu.VMEM((*lead, nt, 8, COLS), f32)

    if kind == "A":
        ring = [block(2, NY // 2), block(2, NY), block(2, NY), block(2, NY)]
        return [block(NZ, NY), *ring, block(NY - 1), dma((13,)), dma((13,))]
    if kind == "B":
        return [block(NY, NZ), block(2, NZ // 2), block(2, NZ), block(NZ - 1), dma((13,)), dma((13,))]
    return [block(NY, NZ), block(NY - 1, NZ), block(NZ - 1), dma((10,)), dma((10,))]


def on_device(
    lesser_hist, greater_hist, advanced_hist, current_row, adjacency, weight_table, step_index
):
    vmem, dma, smem = pltpu.VMEM, pltpu.SemaphoreType.DMA, pltpu.SMEM
    lhs = vmem((HALVES, NS, 2, 2, 4, ROWS, COLS), bf16)
    rhs = vmem((NT // 2, NS, 512, 256), bf16)
    scratch = [
        smem((NS,), jnp.int32),
        smem((1,), jnp.int32),
        vmem((2, NS, ROWS, COLS), f32),
        vmem((2, NS, ROWS, COLS), f32),
        vmem((NT, 2, NS, 256, COLS), f32),
        vmem((2, NT, 8, COLS), f32),
        vmem((8, 256), jnp.int32),
        vmem((HALVES, 8, NS, ROWS, COLS), f32),
        lhs, lhs, rhs, rhs,
        vmem((HALVES, 256, 128), bf16),
        vmem((NT // 2, 128, 256), bf16),
        dma((6,)), dma((NT,)), dma((HALVES, 13)), dma((HALVES, 13)),
    ]
    for stage in STAGES:
        scratch += stage_scratch(stage)
    return pl.pallas_call(
        kernel,
        out_shape=jax.ShapeDtypeStruct((2, NT, 8, COLS), f32),
        in_specs=[pl.BlockSpec(memory_space=pl.ANY)] * 7,
        out_specs=pl.BlockSpec(memory_space=vmem),
        scratch_shapes=scratch,
        compiler_params=pltpu.CompilerParams(
            collective_id=0, has_side_effects=True, vmem_limit_bytes=56 * 1024 * 1024
        ),
        name="row_step",
    )(
        weight_table, step_index, lesser_hist, jnp.swapaxes(greater_hist, 2, 3), advanced_hist,
        current_row, adjacency,
    )


def solution(mesh):
    in_specs = (
        P(None, "hist", "ocol", "orow"),
        P(None, "hist", "orow", "ocol"),
        P(None, "hist", "ocol", None, "orow"),
        P(None, "ocol", "hist", "orow"),
        P("hist", None),
        P("hist"),
        P(),
    )
    out_specs = P(None, "ocol", "hist", "orow")
    return jax.shard_map(
        on_device, mesh=mesh, in_specs=in_specs, out_specs=out_specs, check_vma=False
    )
```

time: 315 us -> 49.7 us (0.16)
  waiting for transfers between devices: 282 us -> 0 us
  Pallas kernels: 0 us -> 47.3 us
  matrix products: 13.4 us -> 0 us
  between operations: 13.8 us -> 0.66 us
  other arithmetic: 4.26 us -> 0 us
    reduce_scatter x1 -> x0, waiting for transfers between devices: 216 us -> none  [on_device(): lax.psum_scatter(collision + hop, 'hist', scatter_dimension=2, tiled=True)]
    all_gather x2 -> x0, waiting for transfers between devices: 65.4 us -> none  [the longest x1 39.4 us: on_device(): sigma = lax.all_gather(sigma, 'orow', axis=3, tiled=True)]
    pallas_call x0 -> x1, Pallas kernels: none -> 47.3 us  [on_device(): pl.pallas_call(kernel, out_shape=jax.ShapeDtypeStruct((2, NT, 8, COLS), f...]
    dot_general x2 -> x0, matrix products: 13.4 us -> none  [the longest x1 10 us: on_device(): jnp.einsum('csik,dstkj->cdtij', sigma, advanced_hist, precision=lax.Preci...]
  transfers between devices with their start and end apart: 3 -> 0, of which waited for: 3 -> 0; matrix products, arithmetic and copies ran while one was open for 0% -> 0% of each run, Pallas kernels for 0% -> 0%
where the time goes in v3:
time: 49.7 us; the launch traced here: 49.4 us
  Pallas kernels  47.3 us (95%)
  local copies, waits for them, and re-layouts  1.47 us (3%)
  between operations  0.66 us (1%)
    pallas_call x1, Pallas kernels, on_device(): pl.pallas_call(kernel, out_shape=jax.ShapeDtypeStruct((2, NT, 8, COLS), f...  47.3 us
    unnamed x1, local copies, waits for them, and re-layouts  1.47 us

profile of v3, /device:TPU:32, one launch (start us, length us, event | category | flops | bytes accessed | tf_op | source)
XLA Modules:
  0.0 49.4 jit_solution(10255128046675056983)
XLA Ops:
  0.7 47.3 %row_step.1 = f32[2,8,8,128]{3,2,1,0:T(8,128)} custom-call(s32[4]{0:T(128)} %table_h.1, s32[1]{0:T(128)S(6)} %copy.9.step_h, f32[2,4,64,128]{3,2,1,0:T(8,128)} %lesser.1, f32[2,4,64,128]{3,2,1,0:T(8,128)} %bitcast.1, f32[2,4,8,256,128]{4,3,2,1,0:T(8,128)} %advanced.1, f32[2,8,8,128]{3,2,1,0:T(8,128)} %row.1, s32[8,256]{1,0:T(8,128)} %adjacency.1), custom_call_target="tpu_custom_call" | custom-call | tf_op jit(solution)/shard_map/row_step/pallas_call | solution.py:486
  47.9 1.5 %copy.10 = f32[2,8,8,128]{3,2,1,0:T(8,128)} copy(f32[2,8,8,128]{3,2,1,0:T(8,128)} %row_step.1) | data formatting | bytes 131072

commit v4 on v3

--- a/solution.py
+++ b/solution.py
@@ -262,9 +262,9 @@
             lambda d=d: (p.at[y, wrap(z + d, NZ)], slots.at[d - 1], dev(dz=d)) for d in range(1, NZ)
         ]
 
-    def ascending(stage, first):
+    def ascending(stage, first, destinations=range(NZ)):
         p, slots = stage.refs[0], stage.refs[-1]
-        for to in range(NZ):
+        for to in destinations:
             @pl.when(z != to)
             def _():
                 d = wrap(to - z, NZ)
@@ -308,9 +308,13 @@
                 self.start(5)
 
             def send():
-                self.got(2, 3, 4, 5)
-                p[y] = p[y] + two[0] + two[1]
-                ascending(self, 6)
+                n = NZ // 2
+                self.got(3, 4)
+                p[y, :n] = p[y, :n] + two[0, :n] + two[1, :n]
+                ascending(self, 6, range(n))
+                self.got(2, 5)
+                p[y, n:] = p[y, n:] + two[0, n:] + two[1, n:]
+                ascending(self, 6, range(n, NZ))
 
             def end():
                 self.got(*range(6, 6 + NZ - 1))

time: 49.7 us -> 49.6 us (level)
  no operation moved by 1% of the time
where the time goes in v4:
time: 49.6 us; the launch traced here: 49.2 us
  Pallas kernels  47.1 us (95%)
  local copies, waits for them, and re-layouts  1.47 us (3%)
  between operations  0.66 us (1%)
    pallas_call x1, Pallas kernels, on_device(): pl.pallas_call(kernel, out_shape=jax.ShapeDtypeStruct((2, NT, 8, COLS), f...  47.1 us
    unnamed x1, local copies, waits for them, and re-layouts  1.47 us

profile of v4, /device:TPU:32, one launch (start us, length us, event | category | flops | bytes accessed | tf_op | source)
XLA Modules:
  0.0 49.2 jit_solution(17042324291502444954)
XLA Ops:
  0.7 47.1 %row_step.1 = f32[2,8,8,128]{3,2,1,0:T(8,128)} custom-call(s32[4]{0:T(128)} %table_h.1, s32[1]{0:T(128)S(6)} %copy.9.step_h, f32[2,4,64,128]{3,2,1,0:T(8,128)} %lesser.1, f32[2,4,64,128]{3,2,1,0:T(8,128)} %bitcast.1, f32[2,4,8,256,128]{4,3,2,1,0:T(8,128)} %advanced.1, f32[2,8,8,128]{3,2,1,0:T(8,128)} %row.1, s32[8,256]{1,0:T(8,128)} %adjacency.1), custom_call_target="tpu_custom_call" | custom-call | tf_op jit(solution)/shard_map/row_step/pallas_call | solution.py:490
  47.7 1.5 %copy.10 = f32[2,8,8,128]{3,2,1,0:T(8,128)} copy(f32[2,8,8,128]{3,2,1,0:T(8,128)} %row_step.1) | data formatting | bytes 131072

commit v5 on v3

--- a/solution.py
+++ b/solution.py
@@ -490,7 +490,7 @@
         out_specs=pl.BlockSpec(memory_space=vmem),
         scratch_shapes=scratch,
         compiler_params=pltpu.CompilerParams(
-            collective_id=0, has_side_effects=True, vmem_limit_bytes=56 * 1024 * 1024
+            collective_id=0, has_side_effects=True, vmem_limit_bytes=55136 * 1024
         ),
         name="row_step",
     )(

time: 49.7 us -> 49.4 us (level)
  Pallas kernels: 47.3 us -> 46.5 us
  local copies, waits for them, and re-layouts: 1.47 us -> 1.98 us
    pallas_call x1, Pallas kernels: 47.3 us -> 46.5 us  [on_device(): pl.pallas_call(kernel, out_shape=jax.ShapeDtypeStruct((2, NT, 8, COLS), f...]
    unnamed x1 -> x5, local copies, waits for them, and re-layouts: 1.47 us -> 1.98 us
where the time goes in v5:
time: 49.4 us; the launch traced here: 49.1 us
  Pallas kernels  46.5 us (94%)
  local copies, waits for them, and re-layouts  1.98 us (4%)
  between operations  0.67 us (1%)
    pallas_call x1, Pallas kernels, on_device(): pl.pallas_call(kernel, out_shape=jax.ShapeDtypeStruct((2, NT, 8, COLS), f...  46.5 us
    unnamed x5, local copies, waits for them, and re-layouts  1.98 us

profile of v5, /device:TPU:32, one launch (start us, length us, event | category | flops | bytes accessed | tf_op | source)
XLA Modules:
  0.0 49.1 jit_solution(10395505901946899158)
XLA Ops:
  0.7 0.0 copy-start
  0.7 0.7 %copy-done = s32[8,256]{1,0:T(8,128)S(1)} copy-done((s32[8,256]{1,0:T(8,128)S(1)}, s32[8,256]{1,0:T(8,128)}, u32[]{:S(2)}) %copy-start) | copy-done | bytes 8216
  1.4 0.0 copy-start.1
  1.4 0.7 %copy-done.1 = s32[4]{0:T(128)S(1)} copy-done((s32[4]{0:T(128)S(1)}, s32[4]{0:T(128)}, u32[]{:S(2)}) %copy-start.1) | copy-done | bytes 40
  2.0 46.5 %row_step.1 = f32[2,8,8,128]{3,2,1,0:T(8,128)S(1)} custom-call(s32[4]{0:T(128)S(1)} %copy-done.1, s32[1]{0:T(128)S(6)} %copy.9.step_h, f32[2,4,64,128]{3,2,1,0:T(8,128)} %lesser.1, f32[2,4,64,128]{3,2,1,0:T(8,128)} %bitcast.1, f32[2,4,8,256,128]{4,3,2,1,0:T(8,128)} %advanced.1, f32[2,8,8,128]{3,2,1,0:T(8,128)} %row.1, s32[8,256]{1,0:T(8,128)S(1)} %copy-done), custom_call_target="tpu_custom_call" | custom-call | tf_op jit(solution)/shard_map/row_step/pallas_call | solution.py:486
  48.5 0.6 %copy.10 = f32[2,8,8,128]{3,2,1,0:T(8,128)} copy(f32[2,8,8,128]{3,2,1,0:T(8,128)S(1)} %row_step.1) | data formatting | bytes 131072
Async XLA Ops:
  0.7 0.7 %copy-start = (s32[8,256]{1,0:T(8,128)S(1)}, s32[8,256]{1,0:T(8,128)}, u32[]{:S(2)}) copy-start(s32[8,256]{1,0:T(8,128)} %adjacency.1) | copy-start | bytes 24580
  1.4 0.7 %copy-start.1 = (s32[4]{0:T(128)S(1)}, s32[4]{0:T(128)}, u32[]{:S(2)}) copy-start(s32[4]{0:T(128)} %table_h.1) | copy-start | bytes 52
